TPU v7x, 32 devices: a whole 2x2x4 slice. The times are simulated.
32 devices in a mesh: face: 2 (over core), sub: 16 (over z, y, x).
Axes of the slice: x: 2, y: 2, z: 4, core: 2. Of those that a mesh axis runs over, the one named last changes fastest.
Arguments:
- features: bfloat16 [768, 24, 192], P(('face', 'sub')), may hold values from -6 to 6
- w_first: bfloat16 [3, 3, 192, 192], replicated, may hold values from -0.15625 to 0.15625
- b_first: float32 [192], replicated, may hold values from -3 to 3
- w_second: bfloat16 [3, 3, 192, 192], replicated, may hold values from -0.15625 to 0.15625
- neighbours: int32 [32, 4], replicated, may hold values from 0 to 31, as said below
- rotations: int32 [32, 4], replicated, may hold values from 0 to 3
- cotangent: bfloat16 [384, 12, 192], P(('face', 'sub')), may hold values from -6 to 6
Outputs:
- pooled: bfloat16 [384, 12, 192], P(('face', 'sub'))
- grad_input: bfloat16 [768, 24, 192], P(('face', 'sub'))
- grad_w1: float32 [3, 3, 192, 192], replicated
- grad_b1: float32 [192], replicated
- grad_w2: float32 [3, 3, 192, 192], replicated
Inputs may be any that keep to these rules, and one draw needn't show every extreme that they name: neighbours[d, e] is a tile f * 16 + s other than d; it has the same f as d or the same s as d; two tiles of the same f share at most one edge, and no tile names the same tile of its own f at two edges.
All inputs are finite; a program needn't handle non-finite values.
Results may differ from a plain program's by a relative error of at most 0.012.
Values may be sent and summed in bfloat16 or wider, within the bound.
A program may use at most 64 MiB of HBM per device.

v0:
```python
import math
import jax
import jax.numpy as jnp
import numpy as np
from jax import lax
from jax.sharding import PartitionSpec as P


def rim_lookup():
    return np.array(
        [
            [[0, 0], [1, 0], [2, 0], [3, 0]],
            [[1, 0], [2, 1], [3, 0], [0, 1]],
            [[2, 1], [3, 1], [0, 1], [1, 1]],
            [[3, 1], [0, 0], [1, 1], [2, 0]],
        ],
        np.int32,
    )


def edge_codes(rotations):
    lookup = rim_lookup()[:, [2, 3, 0, 1], :]
    quarters = rotations[:, :, None] == jnp.arange(4, dtype=jnp.int32)[None, None, :]
    anchor_tab = jnp.asarray(lookup[:, :, 0].T)
    flip_tab = jnp.asarray(lookup[:, :, 1].T)
    anchors = jnp.sum(jnp.where(quarters, anchor_tab[None], 0), axis=2).astype(jnp.int32)
    flip_codes = jnp.sum(jnp.where(quarters, flip_tab[None], 0), axis=2).astype(jnp.int32)
    return (anchors, flip_codes)


def layout(neighbours, rotations):
    sub_count = lax.axis_size("sub")
    face_count = lax.axis_size("face")
    face_id = lax.axis_index("face")
    sub_id = lax.axis_index("sub")
    device = face_id * sub_count + sub_id
    anchors, flip_codes = edge_codes(rotations)

    def by_face(table_in):
        return lax.dynamic_index_in_dim(
            table_in.reshape(face_count, sub_count, 4), sub_id, 1, keepdims=False
        )

    def by_block(table_in):
        return lax.dynamic_slice_in_dim(table_in, face_id * sub_count, sub_count, 0)

    return {
        "device": device,
        "face_id": face_id,
        "sub_count": sub_count,
        "mine_nbr": lax.dynamic_index_in_dim(neighbours, device, 0, keepdims=False),
        "mine_anchor": lax.dynamic_index_in_dim(anchors, device, 0, keepdims=False),
        "mine_flip": lax.dynamic_index_in_dim(flip_codes, device, 0, keepdims=False),
        "block_nbr": by_block(neighbours),
        "block_anchor": by_block(anchors),
        "block_flip": by_block(flip_codes),
        "cross_nbr": by_face(neighbours),
        "cross_anchor": by_face(anchors),
    }


def outer_rows(square):
    return jnp.stack([square[0], square[:, -1], square[-1], square[:, 0]], axis=0)


def border_rows(padded):
    return jnp.stack([padded[0, 1:-1], padded[1:-1, -1], padded[-1, 1:-1], padded[1:-1, 0]], axis=0)


def flip_where(rows_in, flag_vec):
    return jnp.where(flag_vec[:, None, None] == 1, rows_in[:, ::-1], rows_in)


def surround(square, picked):
    padded = jnp.pad(square, ((1, 1), (1, 1), (0, 0)))
    padded = padded.at[0, 1:-1].set(picked[0])
    padded = padded.at[1:-1, -1].set(picked[1])
    padded = padded.at[-1, 1:-1].set(picked[2])
    padded = padded.at[1:-1, 0].set(picked[3])
    return padded


def fetch_halo(square, layout_info):
    extent, channels = (square.shape[0], square.shape[2])
    sub_count = layout_info["sub_count"]
    mine_nbr = layout_info["mine_nbr"]
    mine_anchor = layout_info["mine_anchor"]
    mine_flip = layout_info["mine_flip"]
    same_face = mine_nbr // sub_count == layout_info["face_id"]
    own_rows = outer_rows(square)
    from_face = lax.all_gather(own_rows[None], "face", axis=0, tiled=True).reshape(
        -1, extent * channels
    )
    face_slots = mine_nbr // sub_count * 4 + mine_anchor
    face_pick = (
        face_slots[:, None] == jnp.arange(from_face.shape[0], dtype=jnp.int32)[None, :]
    ) & jnp.logical_not(same_face)[:, None]
    across = jnp.dot(face_pick.astype(jnp.bfloat16), from_face, preferred_element_type=jnp.float32)
    from_block = lax.all_gather(own_rows[None], "sub", axis=0, tiled=True).reshape(
        -1, extent * channels
    )
    block_slots = mine_nbr % sub_count * 4 + mine_anchor
    block_pick = (
        block_slots[:, None] == jnp.arange(from_block.shape[0], dtype=jnp.int32)[None, :]
    ) & same_face[:, None]
    inside = jnp.dot(
        block_pick.astype(jnp.bfloat16), from_block, preferred_element_type=jnp.float32
    )
    picked = flip_where(
        (inside + across).astype(jnp.bfloat16).reshape(4, extent, channels), mine_flip
    )
    return picked


def return_halo(summed, layout_info):
    extent, channels = (summed.shape[0] - 2, summed.shape[2])
    device = layout_info["device"]
    border_ids = jnp.arange(4, dtype=jnp.int32)[None, None, :]
    own_rows = flip_where(border_rows(summed), layout_info["mine_flip"])
    from_face = (
        lax.all_gather(own_rows[None].astype(jnp.bfloat16), "face", axis=0, tiled=True)
        .astype(jnp.float32)
        .reshape(-1, extent * channels)
    )
    cross_mask = (layout_info["cross_nbr"] == device)[:, :, None] & (
        layout_info["cross_anchor"][:, :, None] == border_ids
    )
    arrived = lax.dot_general(
        cross_mask.reshape(-1, 4).astype(jnp.float32),
        from_face,
        (((0,), (0,)), ((), ())),
        precision=lax.Precision.HIGHEST,
        preferred_element_type=jnp.float32,
    )
    block_hits = (layout_info["block_nbr"] == device)[:, :, None] & (
        layout_info["block_anchor"][:, :, None] == border_ids
    )
    from_block = (
        lax.all_gather(own_rows[None].astype(jnp.bfloat16), "sub", axis=0, tiled=True)
        .astype(jnp.float32)
        .reshape(-1, extent * channels)
    )
    block_mask = block_hits.reshape(-1, 4).astype(jnp.float32)
    arrived = arrived + lax.dot_general(
        block_mask,
        from_block,
        (((0,), (0,)), ((), ())),
        precision=lax.Precision.HIGHEST,
        preferred_element_type=jnp.float32,
    )
    arrived = arrived.reshape(4, extent, channels)
    middle = summed[1:-1, 1:-1]
    middle = middle.at[0].add(arrived[0])
    middle = middle.at[:, -1].add(arrived[1])
    middle = middle.at[-1].add(arrived[2])
    middle = middle.at[:, 0].add(arrived[3])
    return middle


def gather_windows(padded, extent):
    portions = []
    for row_off in range(3):
        for col_off in range(3):
            portions.append(
                padded[row_off : row_off + extent, col_off : col_off + extent].reshape(
                    extent * extent, -1
                )
            )
    return jnp.concatenate(portions, axis=1)


def scatter_windows(spread, extent, channels):
    summed = jnp.zeros((extent + 2, extent + 2, channels), jnp.float32)
    for row_off in range(3):
        for col_off in range(3):
            offset_id = 3 * row_off + col_off
            portion = spread[:, offset_id * channels : (offset_id + 1) * channels].reshape(
                extent, extent, channels
            )
            summed = summed.at[row_off : row_off + extent, col_off : col_off + extent].add(portion)
    return summed


def local(features, w_first, b_first, w_second, neighbours, rotations, cotangent):
    extent, channels = (features.shape[1], features.shape[2])
    half_side = extent // 2
    layout_info = layout(neighbours, rotations)
    first_flat = w_first.reshape(9 * channels, channels)
    second_flat = w_second.reshape(9 * channels, channels)
    padded_in = surround(features, fetch_halo(features, layout_info))
    windows_in = gather_windows(padded_in, extent)
    hidden = jnp.dot(windows_in, first_flat, preferred_element_type=jnp.float32) + b_first
    active = jax.nn.silu(hidden).astype(jnp.bfloat16).reshape(extent, extent, channels)
    padded_act = surround(active, fetch_halo(active, layout_info))
    windows_act = gather_windows(padded_act, extent)
    second = jnp.dot(windows_act, second_flat, preferred_element_type=jnp.float32)
    summed_out = features.reshape(extent * extent, channels).astype(jnp.float32) + second
    pooled = (
        summed_out.reshape(half_side, 2, half_side, 2, channels)
        .mean(axis=(1, 3))
        .astype(jnp.bfloat16)
    )
    upward = (cotangent.astype(jnp.float32) * 0.25).astype(jnp.bfloat16)
    grad_out = jnp.broadcast_to(upward[:, None, :, None, :], (half_side, 2, half_side, 2, channels))
    grad_out = grad_out.reshape(extent * extent, channels)
    contract_rows = (((0,), (0,)), ((), ()))
    contract_cols = (((1,), (1,)), ((), ()))
    sum_w2 = lax.dot_general(
        windows_act, grad_out, contract_rows, preferred_element_type=jnp.float32
    )
    spread_two = lax.dot_general(
        grad_out, second_flat, contract_cols, preferred_element_type=jnp.float32
    )
    grad_active = return_halo(scatter_windows(spread_two, extent, channels), layout_info).astype(
        jnp.bfloat16
    )
    sigmoid_h = jax.nn.sigmoid(hidden)
    grad_hidden = (
        grad_active.reshape(extent * extent, channels).astype(jnp.float32)
        * sigmoid_h
        * (1.0 + hidden * (1.0 - sigmoid_h))
    )
    grad_hidden = grad_hidden.astype(jnp.bfloat16)
    sum_b1 = jnp.sum(grad_hidden, axis=0, dtype=jnp.float32)
    sum_w1 = lax.dot_general(
        windows_in, grad_hidden, contract_rows, preferred_element_type=jnp.float32
    )
    spread_one = lax.dot_general(
        grad_hidden, first_flat, contract_cols, preferred_element_type=jnp.float32
    )
    grad_input = return_halo(scatter_windows(spread_one, extent, channels), layout_info)
    grad_input = (
        grad_input + grad_out.astype(jnp.float32).reshape(extent, extent, channels)
    ).astype(jnp.bfloat16)
    total_w1, total_b1, total_w2 = lax.psum((sum_w1, sum_b1, sum_w2), ("face", "sub"))
    grad_scale = 1.0 / math.sqrt(neighbours.shape[0] * extent * extent)
    return (
        pooled,
        grad_input,
        (total_w1 * grad_scale).reshape(3, 3, channels, channels),
        total_b1 * grad_scale,
        (total_w2 * grad_scale).reshape(3, 3, channels, channels),
    )


def solution(mesh):
    in_specs = (
        P(("face", "sub"), None, None),
        P(),
        P(),
        P(),
        P(),
        P(),
        P(("face", "sub"), None, None),
    )
    out_specs = (P(("face", "sub"), None, None), P(("face", "sub"), None, None), P(), P(), P())
    return jax.shard_map(local, mesh=mesh, in_specs=in_specs, out_specs=out_specs, check_vma=False)
```

profile of v0, /device:TPU:0, one launch (start us, length us, event | category | flops | bytes accessed | tf_op | source)
XLA Modules:
  0.0 460.5 jit_solution(812224152784849294)
XLA Ops:
  7.2 1.7 fusion.46
  9.4 1.9 fusion.59
  11.3 2.4 fusion.49
  17.3 6.1 %scatter-add.89 = f32[26,26,192]{2,0,1:T(8,128)S(1)} dynamic-update-slice(f32[26,26,192]{2,0,1:T(8,128)S(1)} %scatter-add.86, f32[24,24,192]{2,0,1:T(8,128)S(1)} %copy_add_fusion.2, s32[]{:T(128)} %bitcast.3, s32[]{:T(128)} %bitcast.4, s32[]{:T(128)} %constant.897.clone.1) | dynamic-update-slice | bytes 884740 | tf_op jit(solution)/shard_map/scatter-add | solution.py:180
  23.4 3.1 add_select_fusion.1
  26.5 6.0 %scatter-add.90 = f32[26,26,192]{2,0,1:T(8,128)S(1)} dynamic-update-slice(f32[26,26,192]{2,0,1:T(8,128)S(1)} %scatter-add.89, f32[24,24,192]{2,0,1:T(8,128)S(1)} %add_select_fusion.1, s32[]{:T(128)} %bitcast.34, s32[]{:T(128)} %bitcast.35, s32[]{:T(128)} %constant.897.clone.1) | dynamic-update-slice | bytes 884740 | tf_op jit(solution)/shard_map/scatter-add | solution.py:180
  33.8 5.1 %scatter-add.91 = f32[26,26,192]{2,0,1:T(8,128)S(1)} dynamic-update-slice(f32[26,26,192]{2,0,1:T(8,128)S(1)} %scatter-add.90, f32[24,24,192]{2,0,1:T(8,128)S(1)} %slice_add_fusion.11, s32[]{:T(128)} %constant.903.clone.1, s32[]{:T(128)} %constant.897.clone.1, s32[]{:T(128)} %constant.897.clone.1) | dynamic-update-slice | bytes 884740 | tf_op jit(solution)/shard_map/scatter-add | solution.py:180
  40.2 4.9 %scatter-add.94 = f32[26,26,192]{2,0,1:T(8,128)S(1)} dynamic-update-slice(f32[26,26,192]{2,0,1:T(8,128)S(1)} %scatter-add.91, f32[24,24,192]{2,0,1:T(8,128)S(1)} %slice_add_fusion.10, s32[]{:T(128)} %constant.903.clone.1, s32[]{:T(128)} %constant.903.clone.1, s32[]{:T(128)} %constant.897.clone.1) | dynamic-update-slice | bytes 884740 | tf_op jit(solution)/shard_map/scatter-add | solution.py:180
  46.4 4.8 %scatter-add.95 = f32[26,26,192]{2,0,1:T(8,128)S(1)} dynamic-update-slice(f32[26,26,192]{2,0,1:T(8,128)S(1)} %scatter-add.94, f32[24,24,192]{2,0,1:T(8,128)S(1)} %slice_add_fusion.9, s32[]{:T(128)} %constant.903.clone.1, s32[]{:T(128)} %constant.911.clone.1, s32[]{:T(128)} %constant.897.clone.1) | dynamic-update-slice | bytes 884740 | tf_op jit(solution)/shard_map/scatter-add | solution.py:180
  52.5 5.1 %scatter-add.96 = f32[26,26,192]{2,0,1:T(8,128)S(1)} dynamic-update-slice(f32[26,26,192]{2,0,1:T(8,128)S(1)} %scatter-add.95, f32[24,24,192]{2,0,1:T(8,128)S(1)} %slice_add_fusion.8, s32[]{:T(128)} %constant.911.clone.1, s32[]{:T(128)} %constant.897.clone.1, s32[]{:T(128)} %constant.897.clone.1) | dynamic-update-slice | bytes 884740 | tf_op jit(solution)/shard_map/scatter-add | solution.py:180
  58.9 4.9 %scatter-add.99 = f32[26,26,192]{2,0,1:T(8,128)S(1)} dynamic-update-slice(f32[26,26,192]{2,0,1:T(8,128)S(1)} %scatter-add.96, f32[24,24,192]{2,0,1:T(8,128)S(1)} %slice_add_fusion.7, s32[]{:T(128)} %constant.911.clone.1, s32[]{:T(128)} %constant.903.clone.1, s32[]{:T(128)} %constant.897.clone.1) | dynamic-update-slice | bytes 884740 | tf_op jit(solution)/shard_map/scatter-add | solution.py:180
  64.1 4.8 %scatter-add.100 = f32[26,26,192]{2,0,1:T(8,128)S(1)} dynamic-update-slice(f32[26,26,192]{2,0,1:T(8,128)S(1)} %scatter-add.99, f32[24,24,192]{2,0,1:T(8,128)S(1)} %slice_add_fusion.6, s32[]{:T(128)} %constant.911.clone.1, s32[]{:T(128)} %constant.911.clone.1, s32[]{:T(128)} %constant.897.clone.1) | dynamic-update-slice | bytes 884740 | tf_op jit(solution)/shard_map/scatter-add | solution.py:180
  70.8 47.0 %all-gather = bf16[64,24,192]{2,1,0:T(8,128)(2,1)S(1)} all-gather(bf16[4,24,192]{2,1,0:T(8,128)(2,1)S(1)} %pad_maximum_fusion.2), channel_id=2, replica_groups=mesh['face'=2,'sub'=16] {'sub'}, dimensions={0}, use_global_device_ids=true | all-gather | bytes 626688 | tf_op jit(solution)/shard_map/all_gather | solution.py:99
  117.8 1.9 all-gather.1
  127.7 39.7 %all-gather.5 = bf16[64,24,192]{2,1,0:T(8,128)(2,1)S(1)} all-gather(bf16[4,24,192]{2,1,0:T(8,128)(2,1)S(1)} %get-tuple-element.535), channel_id=7, replica_groups=mesh['face'=2,'sub'=16] {'sub'}, dimensions={0}, use_global_device_ids=true | all-gather | bytes 626688 | tf_op jit(solution)/shard_map/all_gather | solution.py:139
  167.4 1.9 all-gather.4
  173.7 1.7 fusion.53
  181.9 3.8 concatenate.84
  185.7 3.4 convert_reduce_fusion
  189.1 1.8 copy.330
  196.8 44.8 %all-gather.2 = bf16[64,24,192]{2,1,0:T(8,128)(2,1)} all-gather(bf16[4,24,192]{2,1,0:T(8,128)(2,1)S(1)} %pad_maximum_fusion.3), channel_id=4, replica_groups=mesh['face'=2,'sub'=16] {'sub'}, dimensions={0}, use_global_device_ids=true | all-gather | bytes 626688 | tf_op jit(solution)/shard_map/all_gather | solution.py:99
  241.6 2.0 all-gather.3
  243.6 1.8 fusion.62
  246.2 2.1 fusion.48
  250.0 6.1 %scatter-add.110 = f32[26,26,192]{2,0,1:T(8,128)S(1)} dynamic-update-slice(f32[26,26,192]{2,0,1:T(8,128)S(1)} %scatter-add.109, f32[24,24,192]{2,0,1:T(8,128)S(1)} %copy_add_fusion.1, s32[]{:T(128)} %bitcast.3, s32[]{:T(128)} %bitcast.4, s32[]{:T(128)} %constant.897.clone.1) | dynamic-update-slice | bytes 884740 | tf_op jit(solution)/shard_map/scatter-add | solution.py:180
  256.1 3.1 add_select_fusion
  259.2 6.0 %scatter-add.111 = f32[26,26,192]{2,0,1:T(8,128)S(1)} dynamic-update-slice(f32[26,26,192]{2,0,1:T(8,128)S(1)} %scatter-add.110, f32[24,24,192]{2,0,1:T(8,128)S(1)} %add_select_fusion, s32[]{:T(128)} %bitcast.34, s32[]{:T(128)} %bitcast.35, s32[]{:T(128)} %constant.897.clone.1) | dynamic-update-slice | bytes 884740 | tf_op jit(solution)/shard_map/scatter-add | solution.py:180
  266.5 5.1 %scatter-add.114 = f32[26,26,192]{2,0,1:T(8,128)S(1)} dynamic-update-slice(f32[26,26,192]{2,0,1:T(8,128)S(1)} %scatter-add.111, f32[24,24,192]{2,0,1:T(8,128)S(1)} %slice_add_fusion.5, s32[]{:T(128)} %constant.903.clone.1, s32[]{:T(128)} %constant.897.clone.1, s32[]{:T(128)} %constant.897.clone.1) | dynamic-update-slice | bytes 884740 | tf_op jit(solution)/shard_map/scatter-add | solution.py:180
  272.9 4.9 %scatter-add.115 = f32[26,26,192]{2,0,1:T(8,128)S(1)} dynamic-update-slice(f32[26,26,192]{2,0,1:T(8,128)S(1)} %scatter-add.114, f32[24,24,192]{2,0,1:T(8,128)S(1)} %slice_add_fusion.4, s32[]{:T(128)} %constant.903.clone.1, s32[]{:T(128)} %constant.903.clone.1, s32[]{:T(128)} %constant.897.clone.1) | dynamic-update-slice | bytes 884740 | tf_op jit(solution)/shard_map/scatter-add | solution.py:180
  278.1 4.8 %scatter-add.116 = f32[26,26,192]{2,0,1:T(8,128)S(1)} dynamic-update-slice(f32[26,26,192]{2,0,1:T(8,128)S(1)} %scatter-add.115, f32[24,24,192]{2,0,1:T(8,128)S(1)} %slice_add_fusion.3, s32[]{:T(128)} %constant.903.clone.1, s32[]{:T(128)} %constant.911.clone.1, s32[]{:T(128)} %constant.897.clone.1) | dynamic-update-slice | bytes 884740 | tf_op jit(solution)/shard_map/scatter-add | solution.py:180
  283.1 5.1 %scatter-add.119 = f32[26,26,192]{2,0,1:T(8,128)S(1)} dynamic-update-slice(f32[26,26,192]{2,0,1:T(8,128)S(1)} %scatter-add.116, f32[24,24,192]{2,0,1:T(8,128)S(1)} %slice_add_fusion.2, s32[]{:T(128)} %constant.911.clone.1, s32[]{:T(128)} %constant.897.clone.1, s32[]{:T(128)} %constant.897.clone.1) | dynamic-update-slice | bytes 884740 | tf_op jit(solution)/shard_map/scatter-add | solution.py:180
  288.4 4.9 %scatter-add.120 = f32[26,26,192]{2,0,1:T(8,128)S(1)} dynamic-update-slice(f32[26,26,192]{2,0,1:T(8,128)S(1)} %scatter-add.119, f32[24,24,192]{2,0,1:T(8,128)S(1)} %slice_add_fusion.1, s32[]{:T(128)} %constant.911.clone.1, s32[]{:T(128)} %constant.903.clone.1, s32[]{:T(128)} %constant.897.clone.1) | dynamic-update-slice | bytes 884740 | tf_op jit(solution)/shard_map/scatter-add | solution.py:180
  294.8 4.8 %scatter-add.121 = f32[26,26,192]{2,0,1:T(8,128)S(1)} dynamic-update-slice(f32[26,26,192]{2,0,1:T(8,128)S(1)} %scatter-add.120, f32[24,24,192]{2,0,1:T(8,128)S(1)} %slice_add_fusion, s32[]{:T(128)} %constant.911.clone.1, s32[]{:T(128)} %constant.911.clone.1, s32[]{:T(128)} %constant.897.clone.1) | dynamic-update-slice | bytes 884740 | tf_op jit(solution)/shard_map/scatter-add | solution.py:180
  304.5 1.6 fusion.52
  306.1 3.8 concatenate.85
  309.9 1.8 fusion.61
  312.5 46.0 %all-gather.7 = bf16[64,24,192]{2,1,0:T(8,128)(2,1)} all-gather(bf16[4,24,192]{2,1,0:T(8,128)(2,1)S(1)} %copy-done.9), channel_id=9, replica_groups=mesh['face'=2,'sub'=16] {'sub'}, dimensions={0}, use_global_device_ids=true | all-gather | bytes 626688 | tf_op jit(solution)/shard_map/all_gather | solution.py:139
  358.5 1.9 all-gather.6
  361.3 2.5 reshape.1470
  366.1 1.7 scatter-add.124
  370.1 1.7 scatter-add.126
  377.8 2.1 copy.335
  379.9 2.7 convolution_add_fusion.4
  384.7 37.5 %psum.22 = f32[192]{0:T(256)S(1)} all-reduce(f32[192]{0:T(256)S(1)} %copy-done.34), channel_id=1, replica_groups=mesh['face'=2,'sub'=16] {'face','sub'}, use_global_device_ids=true, to_apply=%region_6.7 | all-reduce | flops 192 | bytes 1536 | tf_op jit(solution)/shard_map/psum | solution.py:235
  423.4 23.8 %all-reduce.7.cloned.1.call-done = (f32[1728,192]{0,1:T(8,128)}, f32[1728,192]{0,1:T(8,128)}) async-done(((f32[1728,192]{0,1:T(8,128)}, f32[1728,192]{0,1:T(8,128)}), (f32[1728,192]{0,1:T(8,128)}, f32[1728,192]{0,1:T(8,128)})) %all-reduce.7.cloned.1.call-update) | async-done | bytes 2654224 | tf_op jit(solution)/shard_map/psum | solution.py:235
  448.6 1.7 copy.370
  450.4 1.5 broadcast_multiply_fusion
  451.9 1.7 copy.371
  (223 shorter events, 66.2 us)
Async XLA Ops:
  7.2 178.5 %copy-start = (bf16[3,3,192,192]{3,2,1,0:T(8,128)(2,1)S(1)}, bf16[3,3,192,192]{3,2,1,0:T(8,128)(2,1)}, u32[]{:S(2)}) copy-start(bf16[3,3,192,192]{3,2,1,0:T(8,128)(2,1)} %param.78) | copy-start | bytes 1990660
  7.2 440.0 %all-reduce.7.cloned.1.call-start = ((), (), s32[]{:S(2)}) async-start(), calls=%async_computation | async-start | bytes 5505024 | tf_op jit(solution)/shard_map/psum | solution.py:235
  13.7 1.5 copy-start.38
  63.8 56.0 %copy-start.31 = (s32[32,4]{0,1:T(4,128)S(1)}, s32[32,4]{0,1:T(4,128)}, u32[]{:S(2)}) copy-start(s32[32,4]{0,1:T(4,128)} %param.82) | copy-start | bytes 1540
  63.8 56.0 %copy-start.32 = (s32[4,4]{1,0:T(4,128)S(1)}, s32[4,4]{1,0:T(4,128)}, u32[]{:S(2)}) copy-start(s32[4,4]{1,0:T(4,128)} %constant.917.clone) | copy-start | bytes 196
  63.9 56.0 %copy-start.33 = (s32[4,4]{1,0:T(4,128)S(1)}, s32[4,4]{1,0:T(4,128)}, u32[]{:S(2)}) copy-start(s32[4,4]{1,0:T(4,128)} %constant.918.clone) | copy-start | bytes 196
  63.9 56.7 %copy-start.17 = (s32[32,4]{0,1:T(4,128)S(1)}, s32[32,4]{0,1:T(4,128)}, u32[]{:S(2)}) copy-start(s32[32,4]{0,1:T(4,128)} %param.81) | copy-start | bytes 1540
  69.0 52.2 %copy-start.11 = (bf16[1,24,192]{2,1,0:T(8,128)(2,1)}, bf16[1,24,192]{2,1,0:T(8,128)(2,1)S(1)}, u32[]{:S(2)}) copy-start(bf16[1,24,192]{2,1,0:T(8,128)(2,1)S(1)} %get-tuple-element.494) | copy-start | bytes 27652
  69.0 52.2 %copy-start.12 = (bf16[1,24,192]{2,1,0:T(8,128)(2,1)}, bf16[1,24,192]{2,1,0:T(8,128)(2,1)S(1)}, u32[]{:S(2)}) copy-start(bf16[1,24,192]{2,1,0:T(8,128)(2,1)S(1)} %get-tuple-element.495) | copy-start | bytes 27652
  119.6 1.6 copy-start.13
  119.7 1.6 copy-start.14
  120.5 0.7 copy-start.15
  121.2 0.6 copy-start.21
  123.1 46.2 %copy-start.16 = (s32[32,4]{0,1:T(4,128)S(1)}, s32[32,4]{0,1:T(4,128)}, u32[]{:S(2)}) copy-start(s32[32,4]{0,1:T(4,128)} %copy-done.15) | copy-start | bytes 1540
  123.1 46.3 %copy-start.18 = (s32[32,4]{0,1:T(4,128)S(1)}, s32[32,4]{0,1:T(4,128)}, u32[]{:S(2)}) copy-start(s32[32,4]{0,1:T(4,128)} %param.81) | copy-start | bytes 1540
  124.0 3.7 copy-start.23
  124.0 3.7 copy-start.36
  126.8 43.7 %copy-start.19 = (pred[4]{0:T(512)(128)(4,1)}, pred[4]{0:T(512)(128)(4,1)S(1)}, u32[]{:S(2)}) copy-start(pred[4]{0:T(512)(128)(4,1)S(1)} %fusion.27) | copy-start | bytes 16
  175.4 4.8 %copy-start.4 = (f32[24,24,192]{2,0,1:T(8,128)S(1)}, f32[24,24,192]{2,0,1:T(8,128)}, u32[]{:S(2)}) copy-start(f32[24,24,192]{2,0,1:T(8,128)} %slice.1244) | copy-start | bytes 1327108
  177.3 2.2 copy-start.27
  177.5 2.1 copy-start.29
  177.8 2.0 copy-start.25
  179.7 2.1 copy-start.7
  181.9 3.8 copy-start.39
  288.4 11.2 %copy-start.6 = (bf16[576,192]{1,0:T(8,128)(2,1)S(1)}, bf16[576,192]{1,0:T(8,128)(2,1)}, u32[]{:S(2)}) copy-start(bf16[576,192]{1,0:T(8,128)(2,1)} %copy.330) | copy-start | bytes 663556
  293.3 6.4 %copy-start.3 = (bf16[64,24,192]{2,1,0:T(8,128)(2,1)S(1)}, bf16[64,24,192]{2,1,0:T(8,128)(2,1)}, u32[]{:S(2)}) copy-start(bf16[64,24,192]{2,1,0:T(8,128)(2,1)} %all-gather.2) | copy-start | bytes 1769476
  294.7 5.7 %copy-start.22 = (pred[4]{0:T(512)(128)(4,1)S(1)}, pred[4]{0:T(512)(128)(4,1)}, u32[]{:S(2)}) copy-start(pred[4]{0:T(512)(128)(4,1)} %get-tuple-element.468) | copy-start | bytes 16
  294.7 5.7 %copy-start.24 = (s32[4]{0:T(128)S(1)}, s32[4]{0:T(128)}, u32[]{:S(2)}) copy-start(s32[4]{0:T(128)} %copy-done.23) | copy-start | bytes 52
  294.8 6.0 %copy-start.10 = (bf16[8,24,192]{2,1,0:T(8,128)(2,1)S(1)}, bf16[8,24,192]{2,1,0:T(8,128)(2,1)}, u32[]{:S(2)}) copy-start(bf16[8,24,192]{2,1,0:T(8,128)(2,1)} %all-gather.3) | copy-start | bytes 221188
  294.8 6.1 %copy-start.35 = (pred[4]{0:T(512)(128)(4,1)S(1)}, pred[4]{0:T(512)(128)(4,1)}, u32[]{:S(2)}) copy-start(pred[4]{0:T(512)(128)(4,1)} %get-tuple-element.467) | copy-start | bytes 16
  294.8 6.1 %copy-start.37 = (s32[4]{0:T(128)S(1)}, s32[4]{0:T(128)}, u32[]{:S(2)}) copy-start(s32[4]{0:T(128)} %copy-done.36) | copy-start | bytes 52
  299.6 1.9 copy-start.20
  311.7 0.8 copy-start.9
  311.7 52.2 %copy-start.28 = (pred[8]{0:T(512)(128)(4,1)S(1)}, pred[8]{0:T(512)(128)(4,1)}, u32[]{:S(2)}) copy-start(pred[8]{0:T(512)(128)(4,1)} %copy-done.27) | copy-start | bytes 28
  311.8 52.2 %copy-start.30 = (s32[8]{0:T(128)S(1)}, s32[8]{0:T(128)}, u32[]{:S(2)}) copy-start(s32[8]{0:T(128)} %copy-done.29) | copy-start | bytes 100
  311.8 52.4 %copy-start.26 = (s32[64]{0:T(128)S(1)}, s32[64]{0:T(128)}, u32[]{:S(2)}) copy-start(s32[64]{0:T(128)} %copy-done.25) | copy-start | bytes 772
  360.4 12.9 %copy-start.8 = (f32[12,12,192]{2,1,0:T(8,128)S(1)}, f32[12,12,192]{2,1,0:T(8,128)}, u32[]{:S(2)}) copy-start(f32[12,12,192]{2,1,0:T(8,128)} %get-tuple-element.523) | copy-start | bytes 331780
  371.8 5.1 %copy-start.5 = (bf16[24,24,192]{2,1,0:T(8,128)(2,1)S(1)}, bf16[24,24,192]{2,1,0:T(8,128)(2,1)}, u32[]{:S(2)}) copy-start(bf16[24,24,192]{2,1,0:T(8,128)(2,1)} %param.77) | copy-start | bytes 663556
  374.6 5.2 %copy-start.2 = (bf16[3,3,192,192]{3,2,1,0:T(8,128)(2,1)S(1)}, bf16[3,3,192,192]{3,2,1,0:T(8,128)(2,1)}, u32[]{:S(2)}) copy-start(bf16[3,3,192,192]{3,2,1,0:T(8,128)(2,1)} %param.80) | copy-start | bytes 1990660
  382.6 2.1 copy-start.34
  450.4 3.3 copy-start.1
Sparse Core Ops, SparseCore 0:
  311.9 135.2 all-reduce.6
where the time goes:
time: 463 us; the launch traced here: 460 us
  blocking collectives  223 us (48%)
  local copies, waits for them, and re-layouts  142 us (31%)
  other arithmetic  39.1 us (8%)
  waiting for transfers between devices  23.8 us (5%)
  matrix products  18 us (4%)
  between operations  15.1 us (3%)
    all_gather x2, blocking collectives, fetch_halo(): lax.all_gather(own_rows[None], 'sub', axis=0, tiled=True)  91.8 us
    all_gather x2, blocking collectives, return_halo(): lax.all_gather(own_rows[None].astype(jnp.bfloat16), 'sub', axis=0, tiled=...  85.7 us
    scatter-add x18, local copies, waits for them, and re-layouts, scatter_windows(): summed.at[row_off:row_off + extent, col_off:col_off + extent].add(portion)  83.3 us
    psum x1, blocking collectives, local(): lax.psum((sum_w1, sum_b1, sum_w2), ('face', 'sub'))  37.5 us
    psum x1, waiting for transfers between devices, local(): lax.psum((sum_w1, sum_b1, sum_w2), ('face', 'sub'))  23.8 us
    add x14, other arithmetic, scatter_windows(): summed.at[row_off:row_off + extent, col_off:col_off + extent].add(portion)  14.4 us
  transfers between devices with their start and end apart: 1, of which 1 were waited for; matrix products, arithmetic and copies ran while one was open for 6% of the time, Pallas kernels for 0%

commit v1 on v0

--- a/solution.py
+++ b/solution.py
@@ -4,6 +4,11 @@
 import numpy as np
 from jax import lax
 from jax.sharding import PartitionSpec as P
+
+
+def by_each_axis(value, inner_axis, outer_axis):
+    partial = lax.psum(value, inner_axis)
+    return lax.psum(partial, outer_axis)
 
 
 def rim_lookup():
@@ -232,7 +237,7 @@
     grad_input = (
         grad_input + grad_out.astype(jnp.float32).reshape(extent, extent, channels)
     ).astype(jnp.bfloat16)
-    total_w1, total_b1, total_w2 = lax.psum((sum_w1, sum_b1, sum_w2), ("face", "sub"))
+    total_w1, total_b1, total_w2 = by_each_axis((sum_w1, sum_b1, sum_w2), "sub", "face")
     grad_scale = 1.0 / math.sqrt(neighbours.shape[0] * extent * extent)
     return (
         pooled,

time: 463 us -> 537 us (1.16)
  waiting for transfers between devices: 23.8 us -> 90.5 us
  blocking collectives: 223 us -> 230 us
    psum x1 -> x2, waiting for transfers between devices: 23.8 us -> 90.5 us  [the longest x1 90.5 us: by_each_axis(): partial = lax.psum(value, inner_axis)]
    psum x1 -> x2, blocking collectives: 37.5 us -> 42.8 us  [the longest x1 40.4 us: by_each_axis(): partial = lax.psum(value, inner_axis)]
  transfers between devices with their start and end apart: 1 -> 2, of which waited for: 1 -> 1; matrix products, arithmetic and copies ran while one was open for 6% -> 5% of each run, Pallas kernels for 0% -> 0%
where the time goes in v1:
time: 537 us; the launch traced here: 535 us
  blocking collectives  230 us (43%)
  local copies, waits for them, and re-layouts  142 us (26%)
  waiting for transfers between devices  90.5 us (17%)
  other arithmetic  39.2 us (7%)
  matrix products  18 us (3%)
  between operations  15.2 us (3%)
    all_gather x2, blocking collectives, fetch_halo(): lax.all_gather(own_rows[None], 'sub', axis=0, tiled=True)  91.8 us
    psum x1, waiting for transfers between devices, by_each_axis(): partial = lax.psum(value, inner_axis)  90.5 us
    all_gather x2, blocking collectives, return_halo(): lax.all_gather(own_rows[None].astype(jnp.bfloat16), 'sub', axis=0, tiled=...  87.6 us
    scatter-add x18, local copies, waits for them, and re-layouts, scatter_windows(): summed.at[row_off:row_off + extent, col_off:col_off + extent].add(portion)  83.4 us
    psum x1, blocking collectives, by_each_axis(): partial = lax.psum(value, inner_axis)  40.4 us
    add x14, other arithmetic, scatter_windows(): summed.at[row_off:row_off + extent, col_off:col_off + extent].add(portion)  14.4 us
  transfers between devices with their start and end apart: 2, of which 1 were waited for; matrix products, arithmetic and copies ran while one was open for 5% of the time, Pallas kernels for 0%

profile of v1, /device:TPU:0, one launch (start us, length us, event | category | flops | bytes accessed | tf_op | source)
XLA Modules:
  0.0 534.7 jit_solution(10737096718554136030)
XLA Ops:
  7.2 1.7 fusion.46
  9.3 1.9 fusion.59
  11.3 2.4 fusion.49
  17.3 6.1 %scatter-add.89 = f32[26,26,192]{2,0,1:T(8,128)S(1)} dynamic-update-slice(f32[26,26,192]{2,0,1:T(8,128)S(1)} %scatter-add.86, f32[24,24,192]{2,0,1:T(8,128)S(1)} %copy_add_fusion.2, s32[]{:T(128)} %bitcast.3, s32[]{:T(128)} %bitcast.4, s32[]{:T(128)} %constant.897.clone.1) | dynamic-update-slice | bytes 884740 | tf_op jit(solution)/shard_map/scatter-add | solution.py:185
  23.4 3.2 add_select_fusion.1
  26.6 6.0 %scatter-add.90 = f32[26,26,192]{2,0,1:T(8,128)S(1)} dynamic-update-slice(f32[26,26,192]{2,0,1:T(8,128)S(1)} %scatter-add.89, f32[24,24,192]{2,0,1:T(8,128)S(1)} %add_select_fusion.1, s32[]{:T(128)} %bitcast.34, s32[]{:T(128)} %bitcast.35, s32[]{:T(128)} %constant.897.clone.1) | dynamic-update-slice | bytes 884740 | tf_op jit(solution)/shard_map/scatter-add | solution.py:185
  33.9 5.1 scatter-add.91
  40.3 4.9 scatter-add.94
  46.5 4.8 scatter-add.95
  52.6 5.1 scatter-add.96
  59.0 4.9 scatter-add.99
  64.2 4.8 scatter-add.100
  70.9 47.0 %all-gather = bf16[64,24,192]{2,1,0:T(8,128)(2,1)S(1)} all-gather(bf16[4,24,192]{2,1,0:T(8,128)(2,1)S(1)} %pad_maximum_fusion.2), channel_id=2, replica_groups=mesh['face'=2,'sub'=16] {'sub'}, dimensions={0}, use_global_device_ids=true | all-gather | bytes 626688 | tf_op jit(solution)/shard_map/all_gather | solution.py:104
  117.9 1.9 all-gather.1
  127.7 39.7 %all-gather.5 = bf16[64,24,192]{2,1,0:T(8,128)(2,1)S(1)} all-gather(bf16[4,24,192]{2,1,0:T(8,128)(2,1)S(1)} %get-tuple-element.537), channel_id=7, replica_groups=mesh['face'=2,'sub'=16] {'sub'}, dimensions={0}, use_global_device_ids=true | all-gather | bytes 626688 | tf_op jit(solution)/shard_map/all_gather | solution.py:144
  167.4 1.9 all-gather.4
  173.7 1.7 fusion.53
  181.9 3.8 concatenate.84
  185.7 3.4 convert_reduce_fusion
  189.0 1.8 copy.330
  196.8 44.8 %all-gather.2 = bf16[64,24,192]{2,1,0:T(8,128)(2,1)} all-gather(bf16[4,24,192]{2,1,0:T(8,128)(2,1)S(1)} %pad_maximum_fusion.3), channel_id=4, replica_groups=mesh['face'=2,'sub'=16] {'sub'}, dimensions={0}, use_global_device_ids=true | all-gather | bytes 626688 | tf_op jit(solution)/shard_map/all_gather | solution.py:104
  241.6 2.0 all-gather.3
  243.6 1.8 fusion.62
  246.2 2.1 fusion.48
  250.0 6.1 %scatter-add.110 = f32[26,26,192]{2,0,1:T(8,128)S(1)} dynamic-update-slice(f32[26,26,192]{2,0,1:T(8,128)S(1)} %scatter-add.109, f32[24,24,192]{2,0,1:T(8,128)S(1)} %copy_add_fusion.1, s32[]{:T(128)} %bitcast.3, s32[]{:T(128)} %bitcast.4, s32[]{:T(128)} %constant.897.clone.1) | dynamic-update-slice | bytes 884740 | tf_op jit(solution)/shard_map/scatter-add | solution.py:185
  256.1 3.2 add_select_fusion
  259.2 6.0 %scatter-add.111 = f32[26,26,192]{2,0,1:T(8,128)S(1)} dynamic-update-slice(f32[26,26,192]{2,0,1:T(8,128)S(1)} %scatter-add.110, f32[24,24,192]{2,0,1:T(8,128)S(1)} %add_select_fusion, s32[]{:T(128)} %bitcast.34, s32[]{:T(128)} %bitcast.35, s32[]{:T(128)} %constant.897.clone.1) | dynamic-update-slice | bytes 884740 | tf_op jit(solution)/shard_map/scatter-add | solution.py:185
  266.6 5.1 scatter-add.114
  273.0 4.9 scatter-add.115
  278.1 4.8 scatter-add.116
  283.2 5.1 scatter-add.119
  288.5 4.9 scatter-add.120
  294.9 4.8 scatter-add.121
  304.6 1.6 fusion.52
  306.2 3.8 concatenate.85
  310.0 1.8 fusion.61
  312.6 1.9 all-gather.6
  314.6 47.9 %all-gather.7 = bf16[64,24,192]{2,1,0:T(8,128)(2,1)} all-gather(bf16[4,24,192]{2,1,0:T(8,128)(2,1)S(1)} %copy-done.9), channel_id=9, replica_groups=mesh['face'=2,'sub'=16] {'sub'}, dimensions={0}, use_global_device_ids=true | all-gather | bytes 626688 | tf_op jit(solution)/shard_map/all_gather | solution.py:144
  362.5 90.5 %all-reduce.9.cloned.1.call-done = (f32[1728,192]{0,1:T(8,128)}, f32[1728,192]{0,1:T(8,128)}) async-done(((f32[1728,192]{0,1:T(8,128)}, f32[1728,192]{0,1:T(8,128)}), (f32[1728,192]{0,1:T(8,128)}, f32[1728,192]{0,1:T(8,128)})) %all-reduce.9.cloned.1.call-update) | async-done | bytes 2654224 | tf_op jit(solution)/shard_map/psum | solution.py:10
  454.2 2.5 reshape.1470
  458.5 1.7 scatter-add.124
  462.6 1.7 scatter-add.126
  470.2 2.1 copy.335
  472.3 2.8 convolution_add_fusion.4
  477.3 40.4 %psum.44 = f32[192]{0:T(256)S(1)} all-reduce(f32[192]{0:T(256)S(1)} %copy-done.34), channel_id=1, replica_groups=mesh['face'=2,'sub'=16] {'sub'}, use_global_device_ids=true, to_apply=%region_7.8 | all-reduce | flops 192 | bytes 1536 | tf_op jit(solution)/shard_map/psum | solution.py:10
  517.7 2.5 psum.45
  522.8 1.7 copy.370
  526.1 1.7 copy.371
  (227 shorter events, 67.9 us)
Async XLA Ops:
  7.2 178.5 %copy-start = (bf16[3,3,192,192]{3,2,1,0:T(8,128)(2,1)S(1)}, bf16[3,3,192,192]{3,2,1,0:T(8,128)(2,1)}, u32[]{:S(2)}) copy-start(bf16[3,3,192,192]{3,2,1,0:T(8,128)(2,1)} %param.78) | copy-start | bytes 1990660
  7.2 445.8 %all-reduce.9.cloned.1.call-start = ((), (), s32[]{:S(2)}) async-start(), calls=%async_computation | async-start | bytes 5505024 | tf_op jit(solution)/shard_map/psum | solution.py:10
  13.7 1.5 copy-start.38
  63.9 56.0 %copy-start.31 = (s32[32,4]{0,1:T(4,128)S(1)}, s32[32,4]{0,1:T(4,128)}, u32[]{:S(2)}) copy-start(s32[32,4]{0,1:T(4,128)} %param.82) | copy-start | bytes 1540
  63.9 56.0 %copy-start.32 = (s32[4,4]{1,0:T(4,128)S(1)}, s32[4,4]{1,0:T(4,128)}, u32[]{:S(2)}) copy-start(s32[4,4]{1,0:T(4,128)} %constant.917.clone) | copy-start | bytes 196
  64.0 56.0 %copy-start.33 = (s32[4,4]{1,0:T(4,128)S(1)}, s32[4,4]{1,0:T(4,128)}, u32[]{:S(2)}) copy-start(s32[4,4]{1,0:T(4,128)} %constant.918.clone) | copy-start | bytes 196
  64.0 56.6 %copy-start.17 = (s32[32,4]{0,1:T(4,128)S(1)}, s32[32,4]{0,1:T(4,128)}, u32[]{:S(2)}) copy-start(s32[32,4]{0,1:T(4,128)} %param.81) | copy-start | bytes 1540
  69.1 52.2 %copy-start.11 = (bf16[1,24,192]{2,1,0:T(8,128)(2,1)}, bf16[1,24,192]{2,1,0:T(8,128)(2,1)S(1)}, u32[]{:S(2)}) copy-start(bf16[1,24,192]{2,1,0:T(8,128)(2,1)S(1)} %get-tuple-element.496) | copy-start | bytes 27652
  69.1 52.2 %copy-start.12 = (bf16[1,24,192]{2,1,0:T(8,128)(2,1)}, bf16[1,24,192]{2,1,0:T(8,128)(2,1)S(1)}, u32[]{:S(2)}) copy-start(bf16[1,24,192]{2,1,0:T(8,128)(2,1)S(1)} %get-tuple-element.497) | copy-start | bytes 27652
  119.7 1.6 copy-start.13
  119.7 1.6 copy-start.14
  120.6 0.7 copy-start.15
  121.3 0.5 copy-start.21
  123.1 46.1 %copy-start.16 = (s32[32,4]{0,1:T(4,128)S(1)}, s32[32,4]{0,1:T(4,128)}, u32[]{:S(2)}) copy-start(s32[32,4]{0,1:T(4,128)} %copy-done.15) | copy-start | bytes 1540
  123.1 46.2 %copy-start.18 = (s32[32,4]{0,1:T(4,128)S(1)}, s32[32,4]{0,1:T(4,128)}, u32[]{:S(2)}) copy-start(s32[32,4]{0,1:T(4,128)} %param.81) | copy-start | bytes 1540
  123.9 3.7 copy-start.25
  124.0 3.7 copy-start.36
  126.8 43.7 %copy-start.19 = (pred[4]{0:T(512)(128)(4,1)}, pred[4]{0:T(512)(128)(4,1)S(1)}, u32[]{:S(2)}) copy-start(pred[4]{0:T(512)(128)(4,1)S(1)} %fusion.27) | copy-start | bytes 16
  175.3 4.8 copy-start.4
  177.3 2.2 copy-start.27
  177.4 2.1 copy-start.29
  177.8 2.0 copy-start.22
  179.7 2.1 copy-start.7
  181.9 3.8 copy-start.39
  288.5 11.2 %copy-start.6 = (bf16[576,192]{1,0:T(8,128)(2,1)S(1)}, bf16[576,192]{1,0:T(8,128)(2,1)}, u32[]{:S(2)}) copy-start(bf16[576,192]{1,0:T(8,128)(2,1)} %copy.330) | copy-start | bytes 663556
  293.4 6.4 %copy-start.3 = (bf16[64,24,192]{2,1,0:T(8,128)(2,1)S(1)}, bf16[64,24,192]{2,1,0:T(8,128)(2,1)}, u32[]{:S(2)}) copy-start(bf16[64,24,192]{2,1,0:T(8,128)(2,1)} %all-gather.2) | copy-start | bytes 1769476
  294.8 5.7 %copy-start.24 = (pred[4]{0:T(512)(128)(4,1)S(1)}, pred[4]{0:T(512)(128)(4,1)}, u32[]{:S(2)}) copy-start(pred[4]{0:T(512)(128)(4,1)} %get-tuple-element.470) | copy-start | bytes 16
  294.8 5.7 %copy-start.26 = (s32[4]{0:T(128)S(1)}, s32[4]{0:T(128)}, u32[]{:S(2)}) copy-start(s32[4]{0:T(128)} %copy-done.25) | copy-start | bytes 52
  294.8 6.0 %copy-start.10 = (bf16[8,24,192]{2,1,0:T(8,128)(2,1)S(1)}, bf16[8,24,192]{2,1,0:T(8,128)(2,1)}, u32[]{:S(2)}) copy-start(bf16[8,24,192]{2,1,0:T(8,128)(2,1)} %all-gather.3) | copy-start | bytes 221188
  294.8 6.1 %copy-start.35 = (pred[4]{0:T(512)(128)(4,1)S(1)}, pred[4]{0:T(512)(128)(4,1)}, u32[]{:S(2)}) copy-start(pred[4]{0:T(512)(128)(4,1)} %get-tuple-element.469) | copy-start | bytes 16
  294.9 6.1 %copy-start.37 = (s32[4]{0:T(128)S(1)}, s32[4]{0:T(128)}, u32[]{:S(2)}) copy-start(s32[4]{0:T(128)} %copy-done.36) | copy-start | bytes 52
  299.6 1.9 copy-start.20
  311.8 0.8 copy-start.9
  311.8 141.1 %copy-start.28 = (pred[8]{0:T(512)(128)(4,1)S(1)}, pred[8]{0:T(512)(128)(4,1)}, u32[]{:S(2)}) copy-start(pred[8]{0:T(512)(128)(4,1)} %copy-done.27) | copy-start | bytes 28
  311.8 141.1 %copy-start.30 = (s32[8]{0:T(128)S(1)}, s32[8]{0:T(128)}, u32[]{:S(2)}) copy-start(s32[8]{0:T(128)} %copy-done.29) | copy-start | bytes 100
  311.9 209.5 %all-reduce.11.cloned.1.call-start = ((), (), s32[]{:S(2)}) async-start(), calls=%async_computation.1 | async-start | bytes 5505024 | tf_op jit(solution)/shard_map/psum | solution.py:11
  452.9 3.7 copy-start.23
  453.0 11.4 %copy-start.8 = (f32[12,12,192]{2,1,0:T(8,128)S(1)}, f32[12,12,192]{2,1,0:T(8,128)}, u32[]{:S(2)}) copy-start(f32[12,12,192]{2,1,0:T(8,128)} %get-tuple-element.525) | copy-start | bytes 331780
  464.3 5.1 copy-start.5
  465.7 6.6 %copy-start.2 = (bf16[3,3,192,192]{3,2,1,0:T(8,128)(2,1)S(1)}, bf16[3,3,192,192]{3,2,1,0:T(8,128)(2,1)}, u32[]{:S(2)}) copy-start(bf16[3,3,192,192]{3,2,1,0:T(8,128)(2,1)} %param.80) | copy-start | bytes 1990660
  475.1 2.2 copy-start.34
  524.5 3.3 copy-start.1
Sparse Core Ops, SparseCore 0:
  312.0 140.9 all-reduce.8
  455.4 22.2 all-reduce.10
